TPU v7x, 32 devices: a whole 2x2x4 slice. The times are simulated.
32 devices in a mesh: groups: 2 (over y), hosts: 8 (over z, x), tensor: 2 (over core).
Axes of the slice: x: 2, y: 2, z: 4, core: 2. Of those that a mesh axis runs over, the one named last changes fastest.
Arguments:
- context_queries: bfloat16 [2048, 8192], P(('groups', 'hosts'), 'tensor'), parts along dimension 0, may hold values from -6 to 6
- context_keys: bfloat16 [2048, 1024], P(('groups', 'hosts'), 'tensor'), parts along dimension 0, may hold values from -6 to 6
- context_values: bfloat16 [2048, 1024], P(('groups', 'hosts'), 'tensor'), parts along dimension 0, may hold values from -6 to 6
- doc_ids: int32 [2048], P(('groups', 'hosts')), parts along dimension 0, may hold values from 0 to 31, never falling along the last dimension, each value on 1 to 128 neighbouring positions
- query_token_rows: bfloat16 [16, 8192], P(('groups', 'hosts'), 'tensor'), parts along dimension 0, may hold values from -6 to 6
- span_start: int32 [16], P(('groups', 'hosts')), parts along dimension 0, may hold values from 0 to 511
Outputs:
- block_out: bfloat16 [2048, 8192], P(('groups', 'hosts'), 'tensor'), parts along dimension 0
- answer: bfloat16 [16, 8192], P(('groups', 'hosts'), 'tensor'), parts along dimension 0
There are 2 independent parts, one for each index of `groups`. A program takes and returns all parts, laid end to end along the dimension named above; each array names one. Nothing has to cross between parts.
All inputs are finite; a program needn't handle non-finite values.
Results may differ from a plain program's by a relative error of at most 0.0043.
Values may be sent and summed in bfloat16 or wider, within the bound.
A program may use at most 64 MiB of HBM per device.

v0:
```python
import jax
import jax.numpy as jnp
from jax import lax
from jax.sharding import PartitionSpec as P

HEAD_SIZE = 128
MASKED_SCORE = -1e30


def from_root(value, axis, source):
    kept = jnp.where(lax.axis_index(axis) == source, value, 0).astype(value.dtype)
    return lax.psum(kept, axis)


def head_groups(matrix, kv_count):
    count_rows = matrix.shape[0]
    return matrix.reshape(
        count_rows, kv_count, matrix.shape[1] // (kv_count * HEAD_SIZE), HEAD_SIZE
    ).transpose(1, 0, 2, 3)


def kv_groups(matrix, kv_count):
    return matrix.reshape(matrix.shape[0], kv_count, HEAD_SIZE).transpose(1, 0, 2)


def block_attention(queries, key_rows, value_rows, visible, factor):
    kv_count = key_rows.shape[1] // HEAD_SIZE

    def block_per_head(operands):
        query_part, key_part, value_part = operands
        scores = (
            jnp.einsum("rgd,sd->rgs", query_part, key_part, preferred_element_type=jnp.float32)
            * factor
        )
        shown = visible[:, None, :]
        peak_score = jnp.max(jnp.where(shown, scores, MASKED_SCORE), -1, keepdims=True)
        weights = jnp.where(shown, jnp.exp(scores - peak_score), 0.0)
        totals = jnp.sum(weights, -1)
        output = jnp.einsum(
            "rgs,sd->rgd",
            weights.astype(jnp.bfloat16),
            value_part,
            preferred_element_type=jnp.float32,
        )
        return (output / totals[..., None]).astype(jnp.bfloat16)

    outputs = lax.map(
        block_per_head,
        (
            head_groups(queries, kv_count),
            kv_groups(key_rows, kv_count),
            kv_groups(value_rows, kv_count),
        ),
    )
    return outputs.transpose(1, 0, 2, 3).reshape(queries.shape[0], queries.shape[1])


def query_partials(queries, key_rows, value_rows, visible, factor):
    kv_count = key_rows.shape[1] // HEAD_SIZE

    def query_per_head(operands):
        query_part, key_part, value_part = operands
        scores = (
            jnp.einsum("qgd,sd->qgs", query_part, key_part, preferred_element_type=jnp.float32)
            * factor
        )
        shown = visible[:, None, :]
        peak_score = jnp.max(jnp.where(shown, scores, MASKED_SCORE), -1)
        weights = jnp.where(shown, jnp.exp(scores - peak_score[..., None]), 0.0)
        totals = jnp.sum(weights, -1)
        partial_acc = jnp.einsum(
            "qgs,sd->qgd",
            weights.astype(jnp.bfloat16),
            value_part,
            preferred_element_type=jnp.float32,
        )
        return (peak_score, totals, partial_acc)

    peaks, totals, accums = lax.map(
        query_per_head,
        (
            head_groups(queries, kv_count),
            kv_groups(key_rows, kv_count),
            kv_groups(value_rows, kv_count),
        ),
    )
    query_count = queries.shape[0]
    peaks = peaks.transpose(1, 0, 2).reshape(query_count, -1)
    totals = totals.transpose(1, 0, 2).reshape(query_count, -1)
    accums = accums.transpose(1, 0, 2, 3).reshape(query_count, -1)
    return (peaks, totals, accums)


def on_device(context_queries, context_keys, context_values, doc_ids, query_token_rows, span_start):
    factor = float(HEAD_SIZE) ** (-0.5)
    host_index = lax.axis_index("hosts")
    host_count = lax.axis_size("hosts")
    block_len = context_queries.shape[0]
    per_host = query_token_rows.shape[0]
    stacked = jnp.stack([context_keys, context_values])
    anchor = from_root(stacked, "hosts", 0)
    key_rows = jnp.concatenate([anchor[0], context_keys], 0)
    value_rows = jnp.concatenate([anchor[1], context_values], 0)
    positions = jnp.arange(block_len, dtype=jnp.int32)
    causal = positions[None, :] <= positions[:, None]
    own_visible = causal & (doc_ids[:, None] == doc_ids[None, :])
    front_visible = jnp.broadcast_to(host_index > 0, (block_len, block_len))
    visible = jnp.concatenate([front_visible, own_visible], 1)
    block_out = block_attention(context_queries, key_rows, value_rows, visible, factor)
    all_queries, all_spans = (
        lax.all_gather(query_token_rows, "hosts", axis=0, tiled=True),
        lax.all_gather(span_start, "hosts", axis=0, tiled=True),
    )
    key_positions = host_index * block_len + positions
    query_visible = key_positions[None, :] >= all_spans[:, None]
    peaks, totals, accums = query_partials(
        all_queries, context_keys, context_values, query_visible, factor
    )
    received = (
        lax.all_to_all(peaks, "hosts", split_axis=0, concat_axis=0, tiled=True),
        lax.all_to_all(totals, "hosts", split_axis=0, concat_axis=0, tiled=True),
        lax.all_to_all(accums, "hosts", split_axis=0, concat_axis=0, tiled=True),
    )
    source_peaks = received[0].reshape(host_count, per_host, -1)
    source_totals = received[1].reshape(host_count, per_host, -1)
    source_accums = received[2].reshape(host_count, per_host, -1)
    overall = jnp.max(source_peaks, 0)
    scales = jnp.exp(source_peaks - overall[None])
    own_totals = jnp.sum(scales * source_totals, 0)
    own_accums = jnp.sum(jnp.repeat(scales, HEAD_SIZE, axis=2) * source_accums, 0)
    answer = (own_accums / jnp.repeat(own_totals, HEAD_SIZE, axis=1)).astype(jnp.bfloat16)
    return (block_out, answer)


def solution(mesh):
    in_specs = (
        P(("groups", "hosts"), "tensor"),
        P(("groups", "hosts"), "tensor"),
        P(("groups", "hosts"), "tensor"),
        P(("groups", "hosts")),
        P(("groups", "hosts"), "tensor"),
        P(("groups", "hosts")),
    )
    out_specs = (P(("groups", "hosts"), "tensor"), P(("groups", "hosts"), "tensor"))
    return jax.shard_map(
        on_device, mesh=mesh, in_specs=in_specs, out_specs=out_specs, check_vma=False
    )
```

profile of v0, /device:TPU:0, one launch (start us, length us, event | category | flops | bytes accessed | tf_op | source)
XLA Modules:
  0.0 166.9 jit_solution(4238791645243524496)
XLA Ops:
  7.2 1.1 copy.26
  9.0 0.6 copy-done.5
  9.6 0.6 dynamic-slice
  10.2 0.8 dynamic-update-slice
  11.1 13.1 %all-reduce.1 = s32[8]{0:T(128)S(1)} all-reduce(s32[8]{0:T(128)S(1)} %dynamic-update-slice), channel_id=1, replica_groups=mesh['groups'=2,'hosts'=8,'tensor'=2] {'hosts'}, use_global_device_ids=true, to_apply=%add.1 | all-reduce | flops 8 | bytes 64
  24.2 30.5 %all-gather = bf16[8,1,4096]{2,1,0:T(2,128)(2,1)S(1)} all-gather(bf16[1,1,4096]{2,1,0:T(2,128)(2,1)S(1)} %bitcast.124), channel_id=1, replica_groups=mesh['groups'=2,'hosts'=8,'tensor'=2] {'hosts'}, dimensions={0}, use_global_device_ids=true | all-gather | bytes 73728 | tf_op jit(solution)/shard_map/all_gather | solution.py:111
  55.1 2.7 %while.26 = (s32[]{:T(128)}, f32[4,8,8]{2,1,0:T(8,128)S(1)}, f32[4,8,8]{2,1,0:T(8,128)S(1)}, f32[4,8,8,128]{3,2,1,0:T(8,128)S(1)}, bf16[4,8,8,128]{3,2,0,1:T(8,1...) while((s32[]{:T(128)}, f32[4,8,8]{2,1,0:T(8,128)S(1)}, ...), condition=%wide.region_8.9_spmd.clone, body=%wide.region_5.8_spmd.clone.sunk | while | flops 4268930 | bytes 241033 | solution.py:79
  57.8 0.7 all_to_all.18
  58.5 3.3 %all-to-all-start = ((f32[8,1,32]{2,1,0:T(1,128)}), f32[8,1,32]{2,1,0:T(1,128)S(1)}, u32[]{:S(2)}, u32[]{:S(2)}) async-start(f32[8,1,32]{2,1,0:T(1,128)} %bitcast.23), calls=%async_computation | async-start | bytes 8192 | tf_op jit(solution)/shard_map/all_to_all | solution.py:120
  61.8 0.7 all_to_all.22
  62.5 5.6 %all-to-all-done = f32[8,1,32]{2,1,0:T(1,128)S(1)} async-done(((f32[8,1,32]{2,1,0:T(1,128)}), f32[8,1,32]{2,1,0:T(1,128)S(1)}, u32[]{:S(2)}, u32[]{:S(2)}) %all-to-all-start) | async-done | bytes 1056 | tf_op jit(solution)/shard_map/all_to_all | solution.py:120
  68.1 3.3 %all-to-all-start.2 = ((f32[8,1,32]{2,1,0:T(1,128)}), f32[8,1,32]{2,1,0:T(1,128)S(1)}, u32[]{:S(2)}, u32[]{:S(2)}) async-start(f32[8,1,32]{2,1,0:T(1,128)} %bitcast.30), calls=%async_computation.2 | async-start | bytes 8192 | tf_op jit(solution)/shard_map/all_to_all | solution.py:121
  71.5 0.7 maximum_select_fusion
  72.3 0.7 copy.39
  72.9 4.9 %all-to-all-done.2 = f32[8,1,32]{2,1,0:T(1,128)S(1)} async-done(((f32[8,1,32]{2,1,0:T(1,128)}), f32[8,1,32]{2,1,0:T(1,128)S(1)}, u32[]{:S(2)}, u32[]{:S(2)}) %all-to-all-start.2) | async-done | bytes 1056 | tf_op jit(solution)/shard_map/all_to_all | solution.py:121
  77.8 3.5 %all-to-all-start.1 = ((f32[8,1,4096]{2,1,0:T(1,128)}), f32[8,1,4096]{2,1,0:T(1,128)S(1)}, u32[]{:S(2)}, u32[]{:S(2)}) async-start(f32[8,1,4096]{2,1,0:T(1,128)} %bitcast.27), calls=%async_computation.1 | async-start | bytes 262144 | tf_op jit(solution)/shard_map/all_to_all | solution.py:122
  81.4 0.7 copy.25
  82.2 6.7 %all-to-all-done.1 = f32[8,1,4096]{2,1,0:T(1,128)S(1)} async-done(((f32[8,1,4096]{2,1,0:T(1,128)}), f32[8,1,4096]{2,1,0:T(1,128)S(1)}, u32[]{:S(2)}, u32[]{:S(2)}) %all-to-all-start.1) | async-done | bytes 131104 | tf_op jit(solution)/shard_map/all_to_all | solution.py:122
  89.3 0.6 divide_convert_fusion
  89.9 58.0 %all-reduce.4.cloned.1.call-done = bf16[2,128,512]{1,2,0:T(8,128)(2,1)} async-done(((bf16[2,128,512]{1,2,0:T(8,128)(2,1)}), bf16[2,128,512]{1,2,0:T(8,128)(2,1)}) %all-reduce.4.cloned.1.call-update) | async-done | bytes 262160 | tf_op jit(solution)/shard_map/psum | solution.py:12
  147.9 1.0 fusion.52
  148.9 0.8 maximum_bitcast_fusion
  149.6 8.3 %while.25 = (s32[]{:T(128)}, bf16[4,128,8,128]{3,1,2,0:T(8,128)(2,1)S(1)}, pred[128,256]{1,0:T(8,128)(4,1)S(1)}, bf16[4,128,8,128]{1,3,2,0:T(8,128)(2,1)S(1)}, b...) while((s32[]{:T(128)}, bf16[4,128,8,128]{3,1,2,0:T(8,128)(2,1)S(1)}, ...), condition=%wide.region_4.5_spmd, body=%wide.region_1.4_spmd.sunk | while | flops 136840704 | bytes 4958285 | solution.py:47
  150.0 0.4 fusion.69
  150.4 1.3 fusion.70
  152.1 0.4 fusion.69
  152.5 1.3 fusion.70
  154.2 0.4 fusion.69
  154.6 1.3 fusion.70
  156.7 1.3 fusion.70
  158.0 0.7 copy.33
  158.7 1.4 copy.53
  (56 shorter events, 5.5 us)
Async XLA Ops:
  7.2 3.7 %copy-start.2 = (bf16[128,512]{1,0:T(8,128)(2,1)S(1)}, bf16[128,512]{1,0:T(8,128)(2,1)}, u32[]{:S(2)}) copy-start(bf16[128,512]{1,0:T(8,128)(2,1)} %param.12) | copy-start | bytes 393220
  8.9 0.7 copy-start.5
  10.9 13.2 %copy-start.3 = (bf16[1,4096]{1,0:T(2,128)(2,1)S(1)}, bf16[1,4096]{1,0:T(2,128)(2,1)}, u32[]{:S(2)}) copy-start(bf16[1,4096]{1,0:T(2,128)(2,1)} %param.14) | copy-start | bytes 24580
  57.8 23.6 %copy-start = (bf16[128,4096]{1,0:T(8,128)(2,1)S(1)}, bf16[128,4096]{1,0:T(8,128)(2,1)}, u32[]{:S(2)}) copy-start(bf16[128,4096]{1,0:T(8,128)(2,1)} %param.10) | copy-start | bytes 3145732
  58.5 9.6 %all-to-all-start = ((f32[8,1,32]{2,1,0:T(1,128)}), f32[8,1,32]{2,1,0:T(1,128)S(1)}, u32[]{:S(2)}, u32[]{:S(2)}) async-start(f32[8,1,32]{2,1,0:T(1,128)} %bitcast.23), calls=%async_computation | async-start | bytes 8192 | tf_op jit(solution)/shard_map/all_to_all | solution.py:120
  68.1 9.6 %all-to-all-start.2 = ((f32[8,1,32]{2,1,0:T(1,128)}), f32[8,1,32]{2,1,0:T(1,128)S(1)}, u32[]{:S(2)}, u32[]{:S(2)}) async-start(f32[8,1,32]{2,1,0:T(1,128)} %bitcast.30), calls=%async_computation.2 | async-start | bytes 8192 | tf_op jit(solution)/shard_map/all_to_all | solution.py:121
  71.5 76.4 %all-reduce.4.cloned.1.call-start = ((), (), s32[]{:S(2)}) async-start(), calls=%async_computation.3 | async-start | bytes 524288 | tf_op jit(solution)/shard_map/psum | solution.py:12
  77.8 3.5 %copy-start.4 = (s32[128]{0:T(128)S(1)}, s32[128]{0:T(128)}, u32[]{:S(2)}) copy-start(s32[128]{0:T(128)} %param.13) | copy-start | bytes 1540
  77.8 11.1 %all-to-all-start.1 = ((f32[8,1,4096]{2,1,0:T(1,128)}), f32[8,1,4096]{2,1,0:T(1,128)S(1)}, u32[]{:S(2)}, u32[]{:S(2)}) async-start(f32[8,1,4096]{2,1,0:T(1,128)} %bitcast.27), calls=%async_computation.1 | async-start | bytes 262144 | tf_op jit(solution)/shard_map/all_to_all | solution.py:122
  82.1 67.5 %copy-start.1 = (bf16[4,128,8,128]{3,1,2,0:T(8,128)(2,1)S(1)}, bf16[4,128,8,128]{3,1,2,0:T(8,128)(2,1)}, u32[]{:S(2)}) copy-start(bf16[4,128,8,128]{3,1,2,0:T(8,128)(2,1)} %custom-call) | copy-start | bytes 3145732
Sparse Core Ops, SparseCore 0:
  75.7 72.1 all-reduce.3
where the time goes:
time: 168 us; the launch traced here: 167 us
  waiting for transfers between devices  75.3 us (45%)
  blocking collectives  43.6 us (26%)
  between operations  14.9 us (9%)
  starting transfers between devices  10.2 us (6%)
  local copies, waits for them, and re-layouts  9.16 us (5%)
  matrix products  8.18 us (5%)
  other arithmetic  5.46 us (3%)
    psum x1, waiting for transfers between devices, from_root(): return lax.psum(kept, axis)  58 us
    all_gather x1, blocking collectives, on_device(): lax.all_gather(query_token_rows, 'hosts', axis=0, tiled=True)  30.5 us
    unnamed x1, blocking collectives  13.1 us
    all_to_all x1, waiting for transfers between devices, on_device(): lax.all_to_all(accums, 'hosts', split_axis=0, concat_axis=0, tiled=True)  6.74 us
    all_to_all x1, waiting for transfers between devices, on_device(): lax.all_to_all(peaks, 'hosts', split_axis=0, concat_axis=0, tiled=True)  5.63 us
    unnamed x20, local copies, waits for them, and re-layouts  5.27 us
    dot_general x4, matrix products, block_per_head(): jnp.einsum('rgs,sd->rgd', weights.astype(jnp.bfloat16), value_part, prefe...  5.21 us
    all_to_all x1, waiting for transfers between devices, on_device(): lax.all_to_all(totals, 'hosts', split_axis=0, concat_axis=0, tiled=True)  4.86 us
  transfers between devices with their start and end apart: 4, of which 4 were waited for; matrix products, arithmetic and copies ran while one was open for 2% of the time, Pallas kernels for 0%

commit v1 on v0

--- a/solution.py
+++ b/solution.py
@@ -9,7 +9,7 @@
 
 def from_root(value, axis, source):
     kept = jnp.where(lax.axis_index(axis) == source, value, 0).astype(value.dtype)
-    return lax.psum(kept, axis)
+    return jnp.sum(lax.all_gather(kept, axis), axis=0)
 
 
 def head_groups(matrix, kv_count):

time: 168 us -> 114 us (0.68)
  waiting for transfers between devices: 75.3 us -> 15.8 us
  other arithmetic: 5.46 us -> 9.87 us
    psum x1 -> x0, waiting for transfers between devices: 58 us -> none  [from_root(): return lax.psum(kept, axis)]
    all_to_all x1, waiting for transfers between devices: 6.74 us -> 4.42 us  [on_device(): lax.all_to_all(accums, 'hosts', split_axis=0, concat_axis=0, tiled=True)]
    reduce_sum x0 -> x1, other arithmetic: none -> 1.97 us  [from_root(): return jnp.sum(lax.all_gather(kept, axis), axis=0)]
    unnamed x20 -> x18, local copies, waits for them, and re-layouts: 5.27 us -> 6.15 us
  transfers between devices with their start and end apart: 4 -> 4, of which waited for: 4 -> 3; matrix products, arithmetic and copies ran while one was open for 2% -> 10% of each run, Pallas kernels for 0% -> 0%
where the time goes in v1:
time: 114 us; the launch traced here: 113 us
  blocking collectives  44.2 us (39%)
  waiting for transfers between devices  15.8 us (14%)
  between operations  14.9 us (13%)
  starting transfers between devices  9.98 us (9%)
  local copies, waits for them, and re-layouts  9.92 us (9%)
  other arithmetic  9.87 us (9%)
  matrix products  8.18 us (7%)
    all_gather x1, blocking collectives, on_device(): lax.all_gather(query_token_rows, 'hosts', axis=0, tiled=True)  31.1 us
    unnamed x1, blocking collectives  13.1 us
    unnamed x18, local copies, waits for them, and re-layouts  6.15 us
    all_to_all x1, waiting for transfers between devices, on_device(): lax.all_to_all(peaks, 'hosts', split_axis=0, concat_axis=0, tiled=True)  5.71 us
    all_to_all x1, waiting for transfers between devices, on_device(): lax.all_to_all(totals, 'hosts', split_axis=0, concat_axis=0, tiled=True)  5.66 us
    dot_general x4, matrix products, block_per_head(): jnp.einsum('rgs,sd->rgd', weights.astype(jnp.bfloat16), value_part, prefe...  5.2 us
    all_to_all x1, waiting for transfers between devices, on_device(): lax.all_to_all(accums, 'hosts', split_axis=0, concat_axis=0, tiled=True)  4.42 us
    all_to_all x1, starting transfers between devices, on_device(): lax.all_to_all(accums, 'hosts', split_axis=0, concat_axis=0, tiled=True)  3.37 us
  transfers between devices with their start and end apart: 4, of which 3 were waited for; matrix products, arithmetic and copies ran while one was open for 10% of the time, Pallas kernels for 0%

profile of v1, /device:TPU:0, one launch (start us, length us, event | category | flops | bytes accessed | tf_op | source)
XLA Modules:
  0.0 113.1 jit_solution(15699147254958061773)
XLA Ops:
  7.2 1.8 %maximum_select_fusion = bf16[1,2,128,512]{3,2,1,0:T(8,128)(2,1)} fusion(bf16[1,1,128,512]{3,2,1,0:T(8,128)(2,1)} %bitcast.115, bf16[1,1,128,512]{3,2,1,0:T(8,128)(2,1)} %bitcast.114, pred[]{:T(512)S(6)} %eq.19), kind=kLoop, calls=%fused_computation.50 | loop fusion | flops 262144 | bytes 524289 | tf_op jit(solution)/shard_map/jit(_where)/select_n | solution.py:11
  9.0 1.0 copy.25
  10.1 1.0 copy.27
  11.8 1.2 %dynamic-slice = u32[1]{0:T(128)} dynamic-slice(u32[32]{0:T(128)} %constant.69, u32[]{:T(128)S(6)} %add.18), dynamic_slice_sizes={1} | dynamic-slice | bytes 12
  13.0 0.8 dynamic-update-slice
  13.8 13.1 %all-reduce.1 = s32[8]{0:T(128)S(1)} all-reduce(s32[8]{0:T(128)S(1)} %dynamic-update-slice), channel_id=1, replica_groups=mesh['groups'=2,'hosts'=8,'tensor'=2] {'hosts'}, use_global_device_ids=true, to_apply=%add.1 | all-reduce | flops 8 | bytes 64
  26.9 31.1 %all-gather = bf16[8,1,4096]{2,1,0:T(2,128)(2,1)S(1)} all-gather(bf16[1,1,4096]{2,1,0:T(2,128)(2,1)} %bitcast.124), channel_id=1, replica_groups=mesh['groups'=2,'hosts'=8,'tensor'=2] {'hosts'}, dimensions={0}, use_global_device_ids=true | all-gather | bytes 73728 | tf_op jit(solution)/shard_map/all_gather | solution.py:111
  58.4 2.7 %while.26 = (s32[]{:T(128)}, f32[4,8,8]{2,1,0:T(8,128)S(1)}, f32[4,8,8]{2,1,0:T(8,128)S(1)}, f32[4,8,8,128]{3,2,1,0:T(8,128)S(1)}, bf16[4,8,8,128]{3,2,0,1:T(8,1...) while((s32[]{:T(128)}, f32[4,8,8]{2,1,0:T(8,128)S(1)}, ...), condition=%wide.region_8.9_spmd.clone, body=%wide.region_5.8_spmd.clone.sunk | while | flops 4268930 | bytes 241033 | solution.py:79
  61.2 0.7 all_to_all.18
  61.9 3.3 %all-to-all-start = ((f32[8,1,32]{2,1,0:T(1,128)}), f32[8,1,32]{2,1,0:T(1,128)S(1)}, u32[]{:S(2)}, u32[]{:S(2)}) async-start(f32[8,1,32]{2,1,0:T(1,128)} %bitcast.23), calls=%async_computation | async-start | bytes 8192 | tf_op jit(solution)/shard_map/all_to_all | solution.py:120
  65.1 0.7 all_to_all.22
  65.8 5.7 %all-to-all-done = f32[8,1,32]{2,1,0:T(1,128)S(1)} async-done(((f32[8,1,32]{2,1,0:T(1,128)}), f32[8,1,32]{2,1,0:T(1,128)S(1)}, u32[]{:S(2)}, u32[]{:S(2)}) %all-to-all-start) | async-done | bytes 1056 | tf_op jit(solution)/shard_map/all_to_all | solution.py:120
  71.5 3.3 %all-to-all-start.2 = ((f32[8,1,32]{2,1,0:T(1,128)}), f32[8,1,32]{2,1,0:T(1,128)S(1)}, u32[]{:S(2)}, u32[]{:S(2)}) async-start(f32[8,1,32]{2,1,0:T(1,128)} %bitcast.30), calls=%async_computation.2 | async-start | bytes 8192 | tf_op jit(solution)/shard_map/all_to_all | solution.py:121
  74.9 0.7 copy.37
  75.5 5.7 %all-to-all-done.2 = f32[8,1,32]{2,1,0:T(1,128)S(1)} async-done(((f32[8,1,32]{2,1,0:T(1,128)}), f32[8,1,32]{2,1,0:T(1,128)S(1)}, u32[]{:S(2)}, u32[]{:S(2)}) %all-to-all-start.2) | async-done | bytes 1056 | tf_op jit(solution)/shard_map/all_to_all | solution.py:121
  81.2 3.4 %all-to-all-start.1 = ((f32[8,1,4096]{2,1,0:T(1,128)}), f32[8,1,4096]{2,1,0:T(1,128)S(1)}, u32[]{:S(2)}, u32[]{:S(2)}) async-start(f32[8,1,4096]{2,1,0:T(1,128)} %bitcast.27), calls=%async_computation.1 | async-start | bytes 262144 | tf_op jit(solution)/shard_map/all_to_all | solution.py:122
  84.7 0.7 copy.23
  85.4 0.6 concatenate.26
  86.0 0.7 reduce_max.27
  86.7 0.7 multiply_reduce_fusion.1
  87.4 4.4 %all-to-all-done.1 = f32[8,1,4096]{2,1,0:T(1,128)S(1)} async-done(((f32[8,1,4096]{2,1,0:T(1,128)}), f32[8,1,4096]{2,1,0:T(1,128)S(1)}, u32[]{:S(2)}, u32[]{:S(2)}) %all-to-all-start.1) | async-done | bytes 131104 | tf_op jit(solution)/shard_map/all_to_all | solution.py:122
  92.2 0.6 divide_convert_fusion
  92.8 2.0 %reduce_sum.50 = bf16[2,128,512]{2,1,0:T(8,128)(2,1)S(1)} reduce(bf16[8,2,128,512]{3,2,1,0:T(8,128)(2,1)} %all-gather.3.cloned.1.call-done, bf16[]{:T(256)} %constant.57.clone.1), dimensions={0}, to_apply=%region_0.1 | reduce | flops 917504 | bytes 2359298 | tf_op jit(solution)/shard_map/reduce_sum | solution.py:12
  95.1 0.8 maximum_bitcast_fusion
  95.8 8.3 %while.25 = (s32[]{:T(128)}, bf16[4,128,8,128]{3,1,2,0:T(8,128)(2,1)S(1)}, pred[128,256]{1,0:T(8,128)(4,1)S(1)}, bf16[4,128,8,128]{1,3,2,0:T(8,128)(2,1)S(1)}, b...) while((s32[]{:T(128)}, bf16[4,128,8,128]{3,1,2,0:T(8,128)(2,1)S(1)}, ...), condition=%wide.region_4.5_spmd, body=%wide.region_1.4_spmd.sunk | while | flops 136840704 | bytes 4958285 | solution.py:47
  96.2 0.4 fusion.69
  96.6 1.3 %fusion.70 = bf16[4,128,8,128]{3,1,2,0:T(8,128)(2,1)S(1)} fusion(bf16[4,128,8,128]{3,1,2,0:T(8,128)(2,1)S(1)} %get-tuple-element.282, s32[]{:T(128)} %get-tuple-element.281, f32[128,8]{0,1:T(8,128)S(1)} %fusion.69, f32[128,8,256]{2,0,1:T(8,128)S(1)} %convolution_multiply_fusion.3, pred[128,256]{1,0:T(8,128)(4,1)S(1)} %get-tuple-element.290, ...), kind=kOutput, calls=%fused_computation.11.clone.1 | convolution fusion | flops 68420864 | bytes 2495488 | tf_op jit(solution)/shard_map/while/body/eval_jaxpr/rgs,sd->rgd/dot_general | solution.py:39
  98.7 1.3 %fusion.70 = bf16[4,128,8,128]{3,1,2,0:T(8,128)(2,1)S(1)} fusion(bf16[4,128,8,128]{3,1,2,0:T(8,128)(2,1)S(1)} %get-tuple-element.282, s32[]{:T(128)} %get-tuple-element.281, f32[128,8]{0,1:T(8,128)S(1)} %fusion.69, f32[128,8,256]{2,0,1:T(8,128)S(1)} %convolution_multiply_fusion.3, pred[128,256]{1,0:T(8,128)(4,1)S(1)} %get-tuple-element.290, ...), kind=kOutput, calls=%fused_computation.11.clone.1 | convolution fusion | flops 68420864 | bytes 2495488 | tf_op jit(solution)/shard_map/while/body/eval_jaxpr/rgs,sd->rgd/dot_general | solution.py:39
  100.8 1.3 %fusion.70 = bf16[4,128,8,128]{3,1,2,0:T(8,128)(2,1)S(1)} fusion(bf16[4,128,8,128]{3,1,2,0:T(8,128)(2,1)S(1)} %get-tuple-element.282, s32[]{:T(128)} %get-tuple-element.281, f32[128,8]{0,1:T(8,128)S(1)} %fusion.69, f32[128,8,256]{2,0,1:T(8,128)S(1)} %convolution_multiply_fusion.3, pred[128,256]{1,0:T(8,128)(4,1)S(1)} %get-tuple-element.290, ...), kind=kOutput, calls=%fused_computation.11.clone.1 | convolution fusion | flops 68420864 | bytes 2495488 | tf_op jit(solution)/shard_map/while/body/eval_jaxpr/rgs,sd->rgd/dot_general | solution.py:39
  102.9 1.3 %fusion.70 = bf16[4,128,8,128]{3,1,2,0:T(8,128)(2,1)S(1)} fusion(bf16[4,128,8,128]{3,1,2,0:T(8,128)(2,1)S(1)} %get-tuple-element.282, s32[]{:T(128)} %get-tuple-element.281, f32[128,8]{0,1:T(8,128)S(1)} %fusion.69, f32[128,8,256]{2,0,1:T(8,128)S(1)} %convolution_multiply_fusion.3, pred[128,256]{1,0:T(8,128)(4,1)S(1)} %get-tuple-element.290, ...), kind=kOutput, calls=%fused_computation.11.clone.1 | convolution fusion | flops 68420864 | bytes 2495488 | tf_op jit(solution)/shard_map/while/body/eval_jaxpr/rgs,sd->rgd/dot_general | solution.py:39
  104.2 0.7 copy.31
  104.9 1.4 %copy.51 = bf16[16,8,32,128]{3,1,2,0:T(8,128)(2,1)} copy(bf16[16,8,32,128]{3,2,1,0:T(8,128)(2,1)S(1)} %bitcast.107) | data formatting | bytes 2097152
  (57 shorter events, 6.4 us)
Async XLA Ops:
  7.2 77.4 %copy-start.4 = (s32[128]{0:T(128)S(1)}, s32[128]{0:T(128)}, u32[]{:S(2)}) copy-start(s32[128]{0:T(128)} %param.13) | copy-start | bytes 1540
  7.2 77.5 %copy-start = (bf16[128,4096]{1,0:T(8,128)(2,1)S(1)}, bf16[128,4096]{1,0:T(8,128)(2,1)}, u32[]{:S(2)}) copy-start(bf16[128,4096]{1,0:T(8,128)(2,1)} %param.10) | copy-start | bytes 3145732
  7.2 85.6 %all-gather.3.cloned.1.call-start = ((), (), s32[]{:S(2)}) async-start(), calls=%async_computation.3 | async-start | bytes 2359296 | tf_op jit(solution)/shard_map/all_gather | solution.py:12
  61.9 9.7 %all-to-all-start = ((f32[8,1,32]{2,1,0:T(1,128)}), f32[8,1,32]{2,1,0:T(1,128)S(1)}, u32[]{:S(2)}, u32[]{:S(2)}) async-start(f32[8,1,32]{2,1,0:T(1,128)} %bitcast.23), calls=%async_computation | async-start | bytes 8192 | tf_op jit(solution)/shard_map/all_to_all | solution.py:120
  71.5 13.1 %copy-start.1 = (f32[8,1,32]{2,1,0:T(1,128)}, f32[8,1,32]{2,1,0:T(1,128)S(1)}, u32[]{:S(2)}) copy-start(f32[8,1,32]{2,1,0:T(1,128)S(1)} %all-to-all-done) | copy-start | bytes 3076
  71.5 9.6 %all-to-all-start.2 = ((f32[8,1,32]{2,1,0:T(1,128)}), f32[8,1,32]{2,1,0:T(1,128)S(1)}, u32[]{:S(2)}, u32[]{:S(2)}) async-start(f32[8,1,32]{2,1,0:T(1,128)} %bitcast.30), calls=%async_computation.2 | async-start | bytes 8192 | tf_op jit(solution)/shard_map/all_to_all | solution.py:121
  81.2 3.5 %copy-start.3 = (f32[8,1,32]{2,1,0:T(1,128)}, f32[8,1,32]{2,1,0:T(1,128)S(1)}, u32[]{:S(2)}) copy-start(f32[8,1,32]{2,1,0:T(1,128)S(1)} %all-to-all-done.2) | copy-start | bytes 3076
  81.2 10.7 %all-to-all-start.1 = ((f32[8,1,4096]{2,1,0:T(1,128)}), f32[8,1,4096]{2,1,0:T(1,128)S(1)}, u32[]{:S(2)}, u32[]{:S(2)}) async-start(f32[8,1,4096]{2,1,0:T(1,128)} %bitcast.27), calls=%async_computation.1 | async-start | bytes 262144 | tf_op jit(solution)/shard_map/all_to_all | solution.py:122
  92.8 3.0 %copy-start.2 = (pred[128,256]{1,0:T(8,128)(4,1)S(1)}, pred[128,256]{1,0:T(8,128)(4,1)}, u32[]{:S(2)}) copy-start(pred[128,256]{1,0:T(8,128)(4,1)} %concatenate.26) | copy-start | bytes 98308
Sparse Core Ops, SparseCore 0:
  10.7 53.2 all-gather.2
